TPU v7x, 32 devices: a whole 2x2x4 slice. The times are simulated.
32 devices in a mesh: groups: 1, gx: 8 (over z, y), gy: 2 (over core), segment: 2 (over x).
Axes of the slice: x: 2, y: 2, z: 4, core: 2. Of those that a mesh axis runs over, the one named last changes fastest.
Arguments:
- activations: bfloat16 [2, 8, 128, 128, 128], P('segment', 'groups', 'gx', 'gy'), may hold values from -6 to 6
- cotangent: bfloat16 [8, 128, 128, 128], P('groups', 'gx', 'gy'), may hold values from -6 to 6
- spectral_weights: float32 [2, 32, 32, 8, 8, 32], P('segment', 'gy', 'gx'), may hold values from -6 to 6
- pointwise: float32 [2, 8, 8], P('segment'), may hold values from -2 to 2
- channel_bias: float32 [2, 8], P('segment'), may hold values from -3 to 3
Outputs:
- input_grads: bfloat16 [2, 8, 128, 128, 128], P('segment', 'groups', 'gx', 'gy')
- spectral_grads: float32 [2, 32, 32, 8, 8, 32], P('segment', 'gy', 'gx', 'groups')
All inputs are finite; a program needn't handle non-finite values.
Results may differ from a plain program's by a relative error of at most 0.0042.
Values may be sent and summed in bfloat16 or wider, within the bound.
A program may use at most 64 MiB of HBM per device.

v0:
```python
import math

import jax
import jax.numpy as jnp
from jax import lax
from jax.sharding import PartitionSpec as P

MODES = 32


highest = lax.Precision.HIGHEST


def from_behind(block, axis, distance):
    devices = range(lax.axis_size(axis))
    route = [(i - distance, i) for i in devices if i - distance in devices]
    return lax.ppermute(block, axis, route)


def trig_basis(length, mode_count):
    half = mode_count // 2
    freqs = jnp.arange(half, dtype=jnp.int32)[:, None]
    points = jnp.arange(length, dtype=jnp.int32)[None, :]
    step_angle = 2.0 * math.pi / length
    cosine = jnp.cos((freqs * points % length).astype(jnp.float32) * step_angle)
    sine = jnp.sin(((freqs + 1) * points % length).astype(jnp.float32) * step_angle)
    rows_all = jnp.concatenate([cosine, sine], axis=0)
    scales = jnp.where(
        jnp.arange(mode_count) == 0, 1.0 / math.sqrt(length), math.sqrt(2.0 / length)
    ).astype(jnp.float32)
    return rows_all * scales[:, None]


def gelu_slope(value):
    normal_cdf = 0.5 * (1.0 + jax.scipy.special.erf(value * 0.7071067811865476))
    return normal_cdf + value * jnp.exp(-0.5 * value * value) * 0.3989422804014327


def channel_mix(matrix, field):
    return jnp.sum(matrix[:, :, None, None, None] * field[None], axis=1)


def body(activations, cotangent, spectral_weights, pointwise, channel_bias):
    inputs = activations[0].astype(jnp.float32)
    channels, rows_x, rows_y, length_z = inputs.shape
    count_x = lax.axis_size("gx")
    count_y = lax.axis_size("gy")
    mode_count = MODES
    along_x = trig_basis(rows_x * count_x, mode_count)
    along_z = trig_basis(length_z, mode_count)
    along_y = lax.dynamic_slice_in_dim(
        trig_basis(rows_y * count_y, mode_count), lax.axis_index("gy") * rows_y, rows_y, 1
    )
    weights = spectral_weights[0]
    mixing = pointwise[0]
    mixing_back = jnp.transpose(mixing)

    def analyse(field):
        third = jnp.einsum("ixyz,cz->cixy", field, along_z, precision=highest)
        partial_value = jnp.einsum(
            "cixy,ax->ciay",
            lax.all_to_all(third, "gx", split_axis=0, concat_axis=2, tiled=True),
            along_x,
            precision=highest,
        )
        return lax.psum_scatter(
            jnp.einsum("ciay,jy->jcia", partial_value, along_y, precision=highest),
            "gy",
            scatter_dimension=0,
            tiled=True,
        )

    def synthesise(spectrum):
        second = jnp.einsum(
            "jcia,jy->ciay",
            lax.all_gather(spectrum, "gy", axis=0, tiled=True),
            along_y,
            precision=highest,
        )
        spread = jnp.einsum("ciay,ax->cixy", second, along_x, precision=highest)
        return jnp.einsum(
            "cixy,cz->ixyz",
            lax.all_to_all(spread, "gx", split_axis=2, concat_axis=0, tiled=True),
            along_z,
            precision=highest,
        )

    input_modes = analyse(inputs)
    mixed = jnp.einsum("jcioa,jcia->jcoa", weights, input_modes, precision=highest)
    pre_act = channel_mix(mixing, inputs)
    pre_act = pre_act + channel_bias[0][:, None, None, None] + synthesise(mixed)
    slope_field = gelu_slope(pre_act)
    segment_index = lax.axis_index("segment")
    segment_count = lax.axis_size("segment")
    incoming = cotangent
    kept_grad = jnp.zeros(cotangent.shape, jnp.bfloat16)
    kept_modes = jnp.zeros(input_modes.shape, jnp.float32)
    for turn_index in range(segment_count):
        active = segment_index == segment_count - 1 - turn_index
        signal = incoming.astype(jnp.float32) * slope_field
        grad_modes = analyse(signal)
        back = jnp.einsum("jcioa,jcoa->jcia", weights, grad_modes, precision=highest)
        input_grad = channel_mix(mixing_back, signal) + synthesise(back)
        input_grad = input_grad.astype(jnp.bfloat16)
        kept_grad = jnp.where(active, input_grad, kept_grad)
        kept_modes = jnp.where(active, grad_modes, kept_modes)
        if turn_index + 1 < segment_count:
            incoming = from_behind(input_grad, "segment", -1)
    weight_grad = jnp.einsum("jcia,jcoa->jcioa", input_modes, kept_modes, precision=highest)
    return (kept_grad[None], weight_grad[None])


def solution(mesh):
    return jax.shard_map(
        body,
        mesh=mesh,
        in_specs=(
            P("segment", "groups", "gx", "gy", None),
            P("groups", "gx", "gy", None),
            P("segment", "gy", "gx", None, None, None),
            P("segment", None, None),
            P("segment", None),
        ),
        out_specs=(
            P("segment", "groups", "gx", "gy", None),
            P("segment", "gy", "gx", "groups", None, None),
        ),
        check_vma=False,
    )
```

profile of v0, /device:TPU:0, one launch (start us, length us, event | category | flops | bytes accessed | tf_op | source)
XLA Modules:
  0.0 441.0 jit_solution(13617722540841769567)
XLA Ops:
  7.4 7.4 %fusion.7 = f32[32,8,16,64]{3,0,2,1:T(8,128)S(1)} fusion(bf16[1,8,16,64,128]{4,3,2,1,0:T(8,128)(2,1)} %param.5, f32[32,128]{1,0:T(8,128)S(1)} %maximum_multiply_fusion), kind=kOutput, calls=%fused_computation.18 | convolution fusion | flops 402653184 | bytes 3162112 | tf_op jit(solution)/shard_map/ixyz,cz->cixy/dot_general | solution.py:59
  18.1 7.3 %all-to-all-start = ((f32[8,1,32768]{2,1,0:T(1,128)}), f32[8,1,32768]{2,1,0:T(1,128)S(1)}, u32[]{:S(2)}, u32[]{:S(2)}) async-start(f32[8,1,32768]{2,1,0:T(1,128)} %reshape.27), calls=%async_computation | async-start | bytes 2097152 | tf_op jit(solution)/shard_map/all_to_all | solution.py:62
  25.4 25.7 %all-to-all-done = f32[8,1,32768]{2,1,0:T(1,128)S(1)} async-done(((f32[8,1,32768]{2,1,0:T(1,128)}), f32[8,1,32768]{2,1,0:T(1,128)S(1)}, u32[]{:S(2)}, u32[]{:S(2)}) %all-to-all-start) | async-done | bytes 1048608 | tf_op jit(solution)/shard_map/all_to_all | solution.py:62
  60.4 7.1 %reduce-scatter.4.cloned.1.call-done = f32[16,4,8,32]{3,0,2,1:T(8,128)} async-done(((f32[32,4,8,32]{3,0,2,1:T(8,128)}), f32[16,4,8,32]{3,0,2,1:T(8,128)}) %reduce-scatter.4.cloned.1.call-update) | async-done | bytes 65552 | tf_op jit(solution)/shard_map/reduce_scatter | solution.py:66
  80.6 5.7 %all-to-all-start.1 = ((f32[8,1,32768]{2,1,0:T(1,128)}), f32[8,1,32768]{2,1,0:T(1,128)}, u32[]{:S(2)}, u32[]{:S(2)}) async-start(f32[8,1,32768]{2,1,0:T(1,128)} %reshape.29), calls=%async_computation.2 | async-start | bytes 2097152 | tf_op jit(solution)/shard_map/all_to_all | solution.py:83
  90.5 7.2 %multiply_reduce_fusion.2 = f32[8,16,64,128]{3,2,1,0:T(8,128)} fusion(f32[8,16,64,128]{3,2,1,0:T(8,128)} %bitcast_convert_fusion, f32[8,8]{1,0:T(8,128)S(1)} %bitcast.160), kind=kLoop, calls=%fused_computation.2 | loop fusion | flops 15728640 | bytes 8388864 | tf_op jit(solution)/shard_map/reduce_sum | solution.py:40
  97.6 15.1 %all-to-all-done.1 = f32[8,1,32768]{2,1,0:T(1,128)} async-done(((f32[8,1,32768]{2,1,0:T(1,128)}), f32[8,1,32768]{2,1,0:T(1,128)}, u32[]{:S(2)}, u32[]{:S(2)}) %all-to-all-start.1) | async-done | bytes 1048608 | tf_op jit(solution)/shard_map/all_to_all | solution.py:83
  122.1 11.8 %convert_multiply_fusion.1 = (f32[8,16,64,128]{3,2,1,0:T(8,128)S(1)}, f32[8,16,64,128]{3,2,1,0:T(8,128)}) fusion(bf16[8,16,64,128]{3,2,1,0:T(8,128)(2,1)} %param.6, f32[32,8,16,64]{3,0,2,1:T(8,128)S(1)} %bitcast.153, f32[32,128]{1,0:T(8,128)S(1)} %maximum_multiply_fusion, f32[8,16,64,128]{3,2,1,0:T(8,128)S(1)} %copy-done.6, f32[8]{0:T(128)S(1)} %bitcast.162), kind=kOutput, calls=%fused_computation.11 | convolution fusion | flops 415236096 | bytes 15745056 | tf_op jit(solution)/shard_map/cixy,cz->ixyz/dot_general | solution.py:81
  133.9 11.3 %fusion.32 = f32[32,8,16,64]{3,0,2,1:T(8,128)S(1)} fusion(f32[8,16,64,128]{3,2,1,0:T(8,128)S(1)} %get-tuple-element.2, f32[32,128]{1,0:T(8,128)S(1)} %maximum_multiply_fusion), kind=kOutput, calls=%fused_computation.54 | convolution fusion | flops 402653184 | bytes 5259264 | tf_op jit(solution)/shard_map/ixyz,cz->cixy/dot_general | solution.py:59
  150.3 29.7 %all_to_all.108 = f32[8,1,32768]{2,1,0:T(1,128)} all-to-all(f32[8,1,32768]{2,1,0:T(1,128)S(1)} %reshape.31), channel_id=1, replica_groups=mesh['groups'=1,'gx'=8,'gy'=2,'segment'=2] {'gx'}, dimensions={0} | all-to-all | bytes 2097152 | tf_op jit(solution)/shard_map/all_to_all | solution.py:62
  192.8 7.1 %reduce-scatter.6.cloned.1.call-done = f32[16,4,8,32]{3,0,2,1:T(8,128)} async-done(((f32[32,4,8,32]{3,0,2,1:T(8,128)}), f32[16,4,8,32]{3,0,2,1:T(8,128)}) %reduce-scatter.6.cloned.1.call-update) | async-done | bytes 65552 | tf_op jit(solution)/shard_map/reduce_scatter | solution.py:66
  213.2 5.7 %all-to-all-start.3 = ((f32[8,1,32768]{2,1,0:T(1,128)}), f32[8,1,32768]{2,1,0:T(1,128)}, u32[]{:S(2)}, u32[]{:S(2)}) async-start(f32[8,1,32768]{2,1,0:T(1,128)} %reshape.33), calls=%async_computation.5 | async-start | bytes 2097152 | tf_op jit(solution)/shard_map/all_to_all | solution.py:83
  219.4 7.2 %multiply_reduce_fusion.1 = f32[8,16,64,128]{3,2,1,0:T(8,128)} fusion(f32[8,16,64,128]{3,2,1,0:T(8,128)} %copy-done.1, f32[8,8]{1,0:T(8,128)S(1)} %copy.49), kind=kLoop, calls=%fused_computation.1 | loop fusion | flops 15728640 | bytes 8388864 | tf_op jit(solution)/shard_map/reduce_sum | solution.py:40
  226.6 18.6 %all-to-all-done.3 = f32[8,1,32768]{2,1,0:T(1,128)} async-done(((f32[8,1,32768]{2,1,0:T(1,128)}), f32[8,1,32768]{2,1,0:T(1,128)}, u32[]{:S(2)}, u32[]{:S(2)}) %all-to-all-start.3) | async-done | bytes 1048608 | tf_op jit(solution)/shard_map/all_to_all | solution.py:83
  245.3 4.3 reduce.9
  254.6 7.1 %add_convert_fusion.1 = bf16[8,16,64,128]{3,2,1,0:T(8,128)(2,1)S(1)} fusion(f32[8,16,64,128]{3,2,1,0:T(8,128)S(1)} %copy-done.4, f32[32,8,16,64]{3,0,2,1:T(8,128)S(1)} %bitcast.152, f32[32,128]{1,0:T(8,128)S(1)} %maximum_multiply_fusion), kind=kOutput, calls=%fused_computation.10 | convolution fusion | flops 404750336 | bytes 7356416 | tf_op jit(solution)/shard_map/cixy,cz->ixyz/dot_general | solution.py:81
  263.1 47.1 %collective-permute-done = bf16[8,16,64,128]{3,2,1,0:T(8,128)(2,1)S(1)} collective-permute-done((bf16[8,16,64,128]{3,2,1,0:T(8,128)(2,1)S(1)}, bf16[8,16,64,128]{3,2,1,0:T(8,128)(2,1)S(1)}, u32[]{:S(2)}, u32[]{:S(2)}) %collective-permute-start) | collective-permute-done | bytes 2097184 | tf_op jit(solution)/shard_map/ppermute | solution.py:17
  311.3 11.3 %fusion.27 = f32[32,8,16,64]{3,0,2,1:T(8,128)S(1)} fusion(f32[8,16,64,128]{3,2,1,0:T(8,128)S(1)} %convert_multiply_fusion, f32[32,128]{1,0:T(8,128)S(1)} %maximum_multiply_fusion), kind=kOutput, calls=%fused_computation.49 | convolution fusion | flops 402653184 | bytes 5259264 | tf_op jit(solution)/shard_map/ixyz,cz->cixy/dot_general | solution.py:59
  327.8 29.7 %all_to_all.109 = f32[8,1,32768]{2,1,0:T(1,128)} all-to-all(f32[8,1,32768]{2,1,0:T(1,128)S(1)} %reshape.35), channel_id=1, replica_groups=mesh['groups'=1,'gx'=8,'gy'=2,'segment'=2] {'gx'}, dimensions={0} | all-to-all | bytes 2097152 | tf_op jit(solution)/shard_map/all_to_all | solution.py:62
  370.4 6.1 %reduce-scatter.8.cloned.1.call-done = f32[16,4,8,32]{3,0,2,1:T(8,128)} async-done(((f32[32,4,8,32]{3,0,2,1:T(8,128)}), f32[16,4,8,32]{3,0,2,1:T(8,128)}) %reduce-scatter.8.cloned.1.call-update) | async-done | bytes 65552 | tf_op jit(solution)/shard_map/reduce_scatter | solution.py:66
  387.6 6.0 %all-to-all-start.5 = ((f32[8,1,32768]{2,1,0:T(1,128)}), f32[8,1,32768]{2,1,0:T(1,128)S(1)}, u32[]{:S(2)}, u32[]{:S(2)}) async-start(f32[8,1,32768]{2,1,0:T(1,128)} %reshape.37), calls=%async_computation.8 | async-start | bytes 2097152 | tf_op jit(solution)/shard_map/all_to_all | solution.py:83
  393.7 7.2 %multiply_reduce_fusion = f32[8,16,64,128]{3,2,1,0:T(8,128)} fusion(f32[8,16,64,128]{3,2,1,0:T(8,128)} %copy-done, f32[8,8]{1,0:T(8,128)S(1)} %copy.49), kind=kLoop, calls=%fused_computation | loop fusion | flops 15728640 | bytes 8388864 | tf_op jit(solution)/shard_map/reduce_sum | solution.py:40
  402.7 17.2 %all-to-all-done.5 = f32[8,1,32768]{2,1,0:T(1,128)S(1)} async-done(((f32[8,1,32768]{2,1,0:T(1,128)}), f32[8,1,32768]{2,1,0:T(1,128)S(1)}, u32[]{:S(2)}, u32[]{:S(2)}) %all-to-all-start.5) | async-done | bytes 1048608 | tf_op jit(solution)/shard_map/all_to_all | solution.py:83
  426.0 8.0 %select_bitcast_fusion = bf16[1,8,16,64,128]{4,3,2,1,0:T(8,128)(2,1)} fusion(bf16[8,16,64,128]{3,2,1,0:T(8,128)(2,1)} %copy-done.7, pred[]{:T(512)S(6)} %eq.24, pred[]{:T(512)S(6)} %eq.22, f32[8,16,64,128]{3,2,1,0:T(8,128)S(1)} %copy-done.3, f32[32,8,16,64]{3,0,2,1:T(8,128)S(1)} %bitcast.151, f32[32,128]{1,0:T(8,128)S(1)} %maximum_multiply_fusion), kind=kOutput, calls=%fused_computation.22 | convolution fusion | flops 406847488 | bytes 9453570 | tf_op jit(solution)/shard_map/cixy,cz->ixyz/dot_general | solution.py:81
  (92 shorter events, 115.1 us)
Async XLA Ops:
  18.1 33.0 %all-to-all-start = ((f32[8,1,32768]{2,1,0:T(1,128)}), f32[8,1,32768]{2,1,0:T(1,128)S(1)}, u32[]{:S(2)}, u32[]{:S(2)}) async-start(f32[8,1,32768]{2,1,0:T(1,128)} %reshape.27), calls=%async_computation | async-start | bytes 2097152 | tf_op jit(solution)/shard_map/all_to_all | solution.py:62
  25.4 42.1 %reduce-scatter.4.cloned.1.call-start = ((), (), s32[]{:S(2)}) async-start(), calls=%async_computation.9 | async-start | bytes 786432 | tf_op jit(solution)/shard_map/reduce_scatter | solution.py:66
  55.9 12.7 %copy-start.2 = (f32[1,16,4,8,8,32]{5,4,3,2,1,0:T(8,128)S(1)}, f32[1,16,4,8,8,32]{5,4,3,2,1,0:T(8,128)}, u32[]{:S(2)}) copy-start(f32[1,16,4,8,8,32]{5,4,3,2,1,0:T(8,128)} %param.7) | copy-start | bytes 1572868
  80.6 32.1 %all-to-all-start.1 = ((f32[8,1,32768]{2,1,0:T(1,128)}), f32[8,1,32768]{2,1,0:T(1,128)}, u32[]{:S(2)}, u32[]{:S(2)}) async-start(f32[8,1,32768]{2,1,0:T(1,128)} %reshape.29), calls=%async_computation.2 | async-start | bytes 2097152 | tf_op jit(solution)/shard_map/all_to_all | solution.py:83
  86.4 4.1 copy-start.10
  86.4 113.6 %reduce-scatter.6.cloned.1.call-start = ((), (), s32[]{:S(2)}) async-start(), calls=%async_computation.10 | async-start | bytes 786432 | tf_op jit(solution)/shard_map/reduce_scatter | solution.py:66
  119.2 2.8 copy-start.6
  119.2 2.8 copy-start.11
  133.9 11.4 %copy-start.1 = (f32[8,16,64,128]{3,2,1,0:T(8,128)}, f32[8,16,64,128]{3,2,1,0:T(8,128)S(1)}, u32[]{:S(2)}) copy-start(f32[8,16,64,128]{3,2,1,0:T(8,128)S(1)} %get-tuple-element.2) | copy-start | bytes 12582916
  213.2 32.1 %all-to-all-start.3 = ((f32[8,1,32768]{2,1,0:T(1,128)}), f32[8,1,32768]{2,1,0:T(1,128)}, u32[]{:S(2)}, u32[]{:S(2)}) async-start(f32[8,1,32768]{2,1,0:T(1,128)} %reshape.33), calls=%async_computation.5 | async-start | bytes 2097152 | tf_op jit(solution)/shard_map/all_to_all | solution.py:83
  218.9 157.6 %reduce-scatter.8.cloned.1.call-start = ((), (), s32[]{:S(2)}) async-start(), calls=%async_computation.11 | async-start | bytes 786432 | tf_op jit(solution)/shard_map/reduce_scatter | solution.py:66
  251.7 2.8 copy-start.4
  254.6 55.7 %copy-start.5 = (f32[8,16,64,128]{3,2,1,0:T(8,128)S(1)}, f32[8,16,64,128]{3,2,1,0:T(8,128)}, u32[]{:S(2)}) copy-start(f32[8,16,64,128]{3,2,1,0:T(8,128)} %get-tuple-element.3) | copy-start | bytes 12582916
  261.6 48.6 %copy-start.7 = (bf16[8,16,64,128]{3,2,1,0:T(8,128)(2,1)}, bf16[8,16,64,128]{3,2,1,0:T(8,128)(2,1)S(1)}, u32[]{:S(2)}) copy-start(bf16[8,16,64,128]{3,2,1,0:T(8,128)(2,1)S(1)} %add_convert_fusion.1) | copy-start | bytes 6291460
  261.6 48.6 %collective-permute-start = (bf16[8,16,64,128]{3,2,1,0:T(8,128)(2,1)S(1)}, bf16[8,16,64,128]{3,2,1,0:T(8,128)(2,1)S(1)}, u32[]{:S(2)}, u32[]{:S(2)}) collective-permute-start(bf16[8,16,64,128]{3,2,1,0:T(8,128)(2,1)S(1)} %add_convert_fusion.1), channel_id=1, source_target_pairs={{1,0},{3,2},{5,4},{7,6},{9,8},{11,10},{13,12},{15,14},{17,16},{19,... | collective-permute-start | bytes 6291464 | tf_op jit(solution)/shard_map/ppermute | solution.py:17
  311.3 11.4 %copy-start = (f32[8,16,64,128]{3,2,1,0:T(8,128)}, f32[8,16,64,128]{3,2,1,0:T(8,128)S(1)}, u32[]{:S(2)}) copy-start(f32[8,16,64,128]{3,2,1,0:T(8,128)S(1)} %convert_multiply_fusion) | copy-start | bytes 12582916
  387.6 32.3 %all-to-all-start.5 = ((f32[8,1,32768]{2,1,0:T(1,128)}), f32[8,1,32768]{2,1,0:T(1,128)S(1)}, u32[]{:S(2)}, u32[]{:S(2)}) async-start(f32[8,1,32768]{2,1,0:T(1,128)} %reshape.37), calls=%async_computation.8 | async-start | bytes 2097152 | tf_op jit(solution)/shard_map/all_to_all | solution.py:83
  393.7 7.2 %copy-start.8 = (f32[16,4,8,32]{3,0,2,1:T(8,128)S(1)}, f32[16,4,8,32]{3,0,2,1:T(8,128)}, u32[]{:S(2)}) copy-start(f32[16,4,8,32]{3,0,2,1:T(8,128)} %reduce-scatter.6.cloned.1.call-done) | copy-start | bytes 196612
  393.7 7.2 %copy-start.9 = (f32[16,4,8,32]{3,0,2,1:T(8,128)S(1)}, f32[16,4,8,32]{3,0,2,1:T(8,128)}, u32[]{:S(2)}) copy-start(f32[16,4,8,32]{3,0,2,1:T(8,128)} %reduce-scatter.8.cloned.1.call-done) | copy-start | bytes 196612
  423.8 2.2 copy-start.3
Sparse Core Ops, SparseCore 0:
  60.5 6.9 reduce-scatter.3
  193.0 6.9 reduce-scatter.5
  370.5 5.9 reduce-scatter.7
where the time goes:
time: 450 us; the launch traced here: 441 us
  waiting for transfers between devices  144 us (32%)
  matrix products  79.5 us (18%)
  blocking collectives  66.3 us (15%)
  local copies, waits for them, and re-layouts  55.7 us (12%)
  other arithmetic  53.9 us (12%)
  starting transfers between devices  26.8 us (6%)
  between operations  14.6 us (3%)
    all_to_all x2, blocking collectives, analyse(): lax.all_to_all(third, 'gx', split_axis=0, concat_axis=2, tiled=True)  59.4 us
    all_to_all x3, waiting for transfers between devices, synthesise(): lax.all_to_all(spread, 'gx', split_axis=2, concat_axis=0, tiled=True)  51 us
    ppermute x1, waiting for transfers between devices, from_behind(): return lax.ppermute(block, axis, route)  47.1 us
    unnamed x39, local copies, waits for them, and re-layouts  32.2 us
    dot_general x3, matrix products, analyse(): third = jnp.einsum('ixyz,cz->cixy', field, along_z, precision=highest)  30.1 us
    dot_general x3, matrix products, synthesise(): jnp.einsum('cixy,cz->ixyz', lax.all_to_all(spread, 'gx', split_axis=2, co...  26.9 us
    all_to_all x1, waiting for transfers between devices, analyse(): lax.all_to_all(third, 'gx', split_axis=0, concat_axis=2, tiled=True)  25.7 us
    reduce_sum x3, other arithmetic, channel_mix(): return jnp.sum(matrix[:, :, None, None, None] * field[None], axis=1)  21.6 us
  transfers between devices with their start and end apart: 8, of which 8 were waited for; matrix products, arithmetic and copies ran while one was open for 6% of the time, Pallas kernels for 0%

commit v1 on v0

v1 whole, which is shorter than its diff:
```python
import functools
import math

import jax
import jax.numpy as jnp
import ml_dtypes
import numpy as np
from jax import lax
from jax.experimental import pallas as pl
from jax.experimental.pallas import tpu as pltpu
from jax.sharding import PartitionSpec as P

MODES = 32
f32, bf16 = jnp.float32, jnp.bfloat16


def from_behind(block, axis, distance):
    devices = range(lax.axis_size(axis))
    route = [(i - distance, i) for i in devices if i - distance in devices]
    return lax.ppermute(block, axis, route)


def trig_basis(length):
    half = MODES // 2
    freqs = np.arange(half)[:, None]
    points = np.arange(length)[None, :]
    step = 2.0 * math.pi / length
    rows = np.concatenate(
        [np.cos((freqs * points % length) * step), np.sin(((freqs + 1) * points % length) * step)]
    )
    scales = np.where(np.arange(MODES) == 0, 1.0 / math.sqrt(length), math.sqrt(2.0 / length))
    return rows * scales[:, None]


def halves(matrix):
    matrix = np.asarray(matrix, np.float32)
    top = matrix.astype(ml_dtypes.bfloat16)
    rest = (matrix - top.astype(np.float32)).astype(ml_dtypes.bfloat16)
    return np.stack([top, rest])


def split(value):
    top = value.astype(bf16)
    return top, (value - top.astype(f32)).astype(bf16)


def dot(a, b, ca=1, cb=0):
    return lax.dot_general(a, b, (((ca,), (cb,)), ((), ())), preferred_element_type=f32)


def kernel(
    back, nx, ny, xr, *refs
):
    if back:
        (inc_ref, slope_ref, w_hbm, mix_ref, bz_ref, bzs_ref, ky_ref, kyt_ref, bx_ref, bxr_ref,
         out_ref, modes_ref, *scratch) = refs
    else:
        (inc_ref, w_hbm, mix_ref, bias_ref, bz_ref, bzs_ref, ky_ref, kyt_ref, bx_ref, bxr_ref,
         out_ref, modes_ref, *scratch) = refs
    (w_ref, sig_ref, ghi_ref, glo_ref, s_ref, r_ref, m_ref, p_ref, q_ref, qs_ref,
     send1, recv1, send2, recv2, wsem) = scratch
    channels, _, yr, zr = inc_ref.shape
    cl, jl, xp = MODES // nx, MODES // ny, r_ref.shape[2]
    n = nx * ny
    lanes = jl * channels
    gx, gy = lax.axis_index("gx"), lax.axis_index("gy")
    me = gx * ny + gy

    wcopy = pltpu.make_async_copy(w_hbm, w_ref, wsem)
    wcopy.start()

    barrier = pltpu.get_barrier_semaphore()

    def greet(k, carry):
        peer = lax.rem(me + k, n)
        pl.semaphore_signal(
            barrier, inc=1,
            device_id={"gx": peer // ny, "gy": lax.rem(peer, ny)},
            device_id_type=pl.DeviceIdType.MESH,
        )
        return carry

    lax.fori_loop(1, n, greet, 0)

    def along_z(x, carry):
        if back:
            signal = inc_ref[:, x].astype(f32) * slope_ref[:, x]
            sig_ref[:, x] = signal
            block = signal.astype(bf16)
        else:
            block = inc_ref[:, x]
        block = block.reshape(channels * yr, zr)
        g = dot(bz_ref[0], block, 1, 1) + dot(bz_ref[1], block, 1, 1)
        ghi, glo = split(g)
        rows = pl.ds(pl.multiple_of(x * MODES, MODES), MODES)
        ghi_ref[rows, :] = ghi
        glo_ref[rows, :] = glo
        return carry

    lax.fori_loop(0, xr, along_z, 0)
    ghi = ghi_ref[...]
    t = dot(ghi, ky_ref[0]) + dot(ghi, ky_ref[1]) + dot(glo_ref[...], ky_ref[0])
    t = jnp.swapaxes(t.reshape(xr, MODES, ny * lanes), 0, 1)
    if xp > xr:
        t = jnp.concatenate([t, jnp.zeros((MODES, xp - xr, ny * lanes), f32)], axis=1)
    t = t.astype(bf16)
    for h in range(ny):
        s_ref[h] = t[:, :, h * lanes : (h + 1) * lanes].reshape(nx, cl, xp, lanes)

    pl.semaphore_wait(barrier, n - 1)

    def exchange(source, target, send, recv):
        def copy_to(peer, slot_of):
            return pltpu.make_async_remote_copy(
                src_ref=source(peer // ny, lax.rem(peer, ny)),
                dst_ref=target.at[lax.rem(slot_of, ny) * nx + slot_of // ny],
                send_sem=send.at[peer],
                recv_sem=recv.at[slot_of],
                device_id={"gx": peer // ny, "gy": lax.rem(peer, ny)},
                device_id_type=pl.DeviceIdType.MESH,
            )

        def begin(k, carry):
            copy_to(lax.rem(me + k, n), me).start()
            return carry

        def finish(k, carry):
            copy_to(lax.rem(me + k, n), me).wait_send()
            peer = lax.rem(me + n - k, n)
            copy_to(peer, peer).wait_recv()
            return carry

        lax.fori_loop(1, n, begin, 0)
        target[gy * nx + gx] = source(gx, gy)[...]
        lax.fori_loop(1, n, finish, 0)

    exchange(lambda d, h: s_ref.at[h, d], r_ref, send1, recv1)

    for c in range(cl):
        part = r_ref[:, c].reshape(n * xp, lanes)
        own = dot(bx_ref[0], part) + dot(bx_ref[1], part)
        modes_ref[c] = own.T.reshape(jl, channels, MODES)
    wcopy.wait()

    def mix(j, carry):
        for c in range(cl):
            own = modes_ref[c, j]
            weight = w_ref[j, c]
            if back:
                m_ref[c, j] = jnp.sum(weight * own[None], axis=1)
            else:
                m_ref[c, j] = jnp.sum(weight * own[:, None, :], axis=0)
        return carry

    lax.fori_loop(0, jl, mix, 0)
    for c in range(cl):
        top, rest = split(m_ref[c].reshape(lanes, MODES))
        spread = (
            dot(bxr_ref[0], top, 1, 1) + dot(bxr_ref[1], top, 1, 1) + dot(bxr_ref[0], rest, 1, 1)
        )
        p_ref[:, c] = spread.astype(bf16).reshape(nx, xp, lanes)

    exchange(lambda d, h: p_ref.at[d], q_ref, send2, recv2)

    got = [q_ref[h * nx : (h + 1) * nx].reshape(MODES, xp, lanes) for h in range(ny)]
    got = jnp.concatenate(got, axis=2).astype(f32)
    got = jnp.swapaxes(got, 0, 1)[:xr].reshape(xr * MODES, ny * lanes).astype(bf16)
    qs_ref[...] = dot(got, kyt_ref[0]) + dot(got, kyt_ref[1])

    def finish_field(x, carry):
        rows = pl.ds(pl.multiple_of(x * MODES, MODES), MODES)
        top, rest = split(qs_ref[rows, :])
        stack = jnp.concatenate([top, rest, top], axis=0)
        field = dot(stack, bzs_ref[...], 0, 0).reshape(channels, yr, zr)
        if back:
            values = [sig_ref[i, x] for i in range(channels)]
        else:
            values = [inc_ref[i, x].astype(f32) for i in range(channels)]
        for o in range(channels):
            total = field[o]
            for i in range(channels):
                total = total + (mix_ref[i, o] if back else mix_ref[o, i]) * values[i]
            if back:
                out_ref[o, x] = total.astype(bf16)
            else:
                total = total + bias_ref[0, o]
                cdf = 0.5 * (1.0 + lax.erf(total * 0.7071067811865476))
                out_ref[o, x] = cdf + total * jnp.exp(-0.5 * total * total) * 0.3989422804014327
        return carry

    lax.fori_loop(0, xr, finish_field, 0)


def block_turn(back, nx, ny, collective, field, slope, weights, mixing, bias, tables):
    channels, xr, yr, zr = field.shape
    xp = -(-xr // 16) * 16
    cl, jl, n = MODES // nx, MODES // ny, nx * ny
    lanes = jl * channels
    vmem = pl.BlockSpec(memory_space=pltpu.VMEM)
    smem = pl.BlockSpec(memory_space=pltpu.SMEM)
    hbm = pl.BlockSpec(memory_space=pl.ANY)
    if back:
        args = (field, slope, weights, mixing, *tables)
        specs = [vmem, vmem, hbm, smem] + [vmem] * len(tables)
    else:
        args = (field, weights, mixing, bias, *tables)
        specs = [vmem, hbm, smem, smem] + [vmem] * len(tables)
    dma = pltpu.SemaphoreType.DMA
    return pl.pallas_call(
        functools.partial(kernel, back, nx, ny, xr),
        out_shape=(
            jax.ShapeDtypeStruct(field.shape, bf16 if back else f32),
            jax.ShapeDtypeStruct((cl, jl, channels, MODES), f32),
        ),
        in_specs=specs,
        out_specs=(vmem, vmem),
        scratch_shapes=[
            pltpu.VMEM(weights.shape, f32),
            pltpu.VMEM(field.shape if back else (8, 128), f32),
            pltpu.VMEM((xr * MODES, channels * yr), bf16),
            pltpu.VMEM((xr * MODES, channels * yr), bf16),
            pltpu.VMEM((ny, nx, cl, xp, lanes), bf16),
            pltpu.VMEM((n, cl, xp, lanes), bf16),
            pltpu.VMEM((cl, jl, channels, MODES), f32),
            pltpu.VMEM((nx, cl, xp, lanes), bf16),
            pltpu.VMEM((n, cl, xp, lanes), bf16),
            pltpu.VMEM((xr * MODES, channels * yr), f32),
            dma((n,)), dma((n,)), dma((n,)), dma((n,)), dma,
        ],
        compiler_params=pltpu.CompilerParams(
            collective_id=collective, has_side_effects=True, vmem_limit_bytes=50 * 2**20
        ),
        cost_estimate=pl.CostEstimate(flops=10**9, bytes_accessed=2 * 10**7, transcendentals=10**6),
    )(*args)


def body(activations, cotangent, spectral_weights, pointwise, channel_bias):
    inputs = activations[0]
    channels, xr, yr, zr = inputs.shape
    nx, ny = lax.axis_size("gx"), lax.axis_size("gy")
    xp = -(-xr // 16) * 16
    bz = trig_basis(zr)
    bx = trig_basis(xr * nx).reshape(MODES, nx, xr)
    bx = np.concatenate([bx, np.zeros((MODES, nx, xp - xr))], axis=2).reshape(MODES, nx * xp)
    by = trig_basis(yr * ny).reshape(MODES, ny, yr)
    kron = np.einsum("jgy,ik->giyjk", by, np.eye(channels)).reshape(
        ny, channels * yr, MODES * channels
    )
    bzh = halves(bz)
    kh = halves(kron)
    gy = lax.axis_index("gy")
    ky = lax.dynamic_index_in_dim(jnp.asarray(np.swapaxes(kh, 0, 1)), gy, 0, False)
    kyt = lax.dynamic_index_in_dim(
        jnp.asarray(np.ascontiguousarray(np.transpose(kh, (1, 0, 3, 2)))), gy, 0, False
    )
    tables = (
        jnp.asarray(bzh),
        jnp.asarray(np.concatenate([bzh[0], bzh[0], bzh[1]], axis=0)),
        ky,
        kyt,
        jnp.asarray(halves(np.concatenate([bx] * ny, axis=1))),
        jnp.asarray(halves(bx.T)),
    )
    weights = spectral_weights[0]
    mixing = pointwise[0]
    slope, input_modes = block_turn(
        False, nx, ny, 0, inputs, None, weights, mixing, channel_bias, tables
    )
    segment_index = lax.axis_index("segment")
    segment_count = lax.axis_size("segment")
    incoming = cotangent
    kept_grad = jnp.zeros(cotangent.shape, bf16)
    kept_modes = jnp.zeros(input_modes.shape, f32)
    for turn_index in range(segment_count):
        active = segment_index == segment_count - 1 - turn_index
        input_grad, grad_modes = block_turn(
            True, nx, ny, 1 + turn_index, incoming, slope, weights, mixing, None, tables
        )
        kept_grad = jnp.where(active, input_grad, kept_grad)
        kept_modes = jnp.where(active, grad_modes, kept_modes)
        if turn_index + 1 < segment_count:
            incoming = from_behind(input_grad, "segment", -1)
    input_modes = jnp.swapaxes(input_modes, 0, 1)
    kept_modes = jnp.swapaxes(kept_modes, 0, 1)
    weight_grad = input_modes[:, :, :, None, :] * kept_modes[:, :, None, :, :]
    return (kept_grad[None], weight_grad[None])


def solution(mesh):
    return jax.shard_map(
        body,
        mesh=mesh,
        in_specs=(
            P("segment", "groups", "gx", "gy", None),
            P("groups", "gx", "gy", None),
            P("segment", "gy", "gx", None, None, None),
            P("segment", None, None),
            P("segment", None),
        ),
        out_specs=(
            P("segment", "groups", "gx", "gy", None),
            P("segment", "gy", "gx", "groups", None, None),
        ),
        check_vma=False,
    )
```

time: 450 us -> 152 us (0.34); the launches traced: 441 us -> 152 us
  waiting for transfers between devices: 144 us -> 49 us
  Pallas kernels: 0 us -> 91.1 us
  matrix products: 79.5 us -> 0 us
  blocking collectives: 66.3 us -> 0 us
  other arithmetic: 53.9 us -> 3.23 us
  local copies, waits for them, and re-layouts: 55.7 us -> 6.04 us
  starting transfers between devices: 26.8 us -> 1.28 us
  between operations: 14.6 us -> 0.79 us
    pallas_call x0 -> x3, Pallas kernels: none -> 91.1 us  [block_turn(): pl.pallas_call(functools.partial(kernel, back, nx, ny, xr), out_shape=(ja...]
    dot_general x18 -> x0, matrix products: 79.5 us -> none  [the longest x3 30.1 us: analyse(): third = jnp.einsum('ixyz,cz->cixy', field, along_z, precision=highest)]
    all_to_all x4 -> x0, waiting for transfers between devices: 76.7 us -> none  [the longest x3 51 us: synthesise(): lax.all_to_all(spread, 'gx', split_axis=2, concat_axis=0, tiled=True)]
    all_to_all x2 -> x0, blocking collectives: 59.4 us -> none  [analyse(): lax.all_to_all(third, 'gx', split_axis=0, concat_axis=2, tiled=True)]
    unnamed x39 -> x26, local copies, waits for them, and re-layouts: 32.2 us -> 3.73 us
    all_to_all x4 -> x0, starting transfers between devices: 24.8 us -> none  [the longest x3 17.5 us: synthesise(): lax.all_to_all(spread, 'gx', split_axis=2, concat_axis=0, tiled=True)]
    all_to_all x6 -> x0, other arithmetic: 23.5 us -> none  [the longest x3 11.8 us: synthesise(): lax.all_to_all(spread, 'gx', split_axis=2, concat_axis=0, tiled=True)]
    reduce_sum x3 -> x0, other arithmetic: 21.6 us -> none  [channel_mix(): return jnp.sum(matrix[:, :, None, None, None] * field[None], axis=1)]
  transfers between devices with their start and end apart: 8 -> 1, of which waited for: 8 -> 1; matrix products, arithmetic and copies ran while one was open for 6% -> 0% of each run, Pallas kernels for 0% -> 0%
where the time goes in v1:
time: 152 us
  Pallas kernels  91.1 us (60%)
  waiting for transfers between devices  49 us (32%)
  local copies, waits for them, and re-layouts  6.04 us (4%)
  other arithmetic  3.23 us (2%)
    pallas_call x3, Pallas kernels, block_turn(): pl.pallas_call(functools.partial(kernel, back, nx, ny, xr), out_shape=(ja...  91.1 us
    ppermute x1, waiting for transfers between devices, from_behind(): return lax.ppermute(block, axis, route)  49 us
    unnamed x26, local copies, waits for them, and re-layouts  3.73 us
  transfers between devices with their start and end apart: 1, of which 1 were waited for; matrix products, arithmetic and copies ran while one was open for 0% of the time, Pallas kernels for 0%

profile of v1, /device:TPU:0, one launch (start us, length us, event | category | flops | bytes accessed | tf_op | source)
XLA Modules:
  0.0 151.5 jit_solution(12815737817569772764)
XLA Ops:
  0.6 0.0 copy-start.7
  0.6 0.0 copy-start
  0.7 0.0 copy-start.12
  0.7 1.2 dynamic-slice_bitcast_fusion.refs_7_
  1.9 1.1 dynamic-slice_bitcast_fusion.1.refs_6_
  3.0 0.0 copy-done.7
  3.0 0.0 copy-done
  3.0 0.0 copy-done.12
  3.0 0.0 copy-start.1
  3.0 0.8 copy-done.1
  3.9 0.8 copy-done.3
  4.6 0.7 copy-done.8
  5.3 0.7 copy-done.10
  6.0 31.4 %shard_map.122 = (f32[8,16,64,128]{3,2,1,0:T(8,128)}, f32[4,16,8,32]{3,2,1,0:T(8,128)S(1)}) custom-call(bf16[8,16,64,128]{3,2,1,0:T(8,128)(2,1)S(1)} %bitcast.15, f32[16,4,8,8,32]{4,3,2,1,0:T(8,128)} %bitcast.19, f32[8,8]{1,0:T(8,128)S(1)} %bitcast.16, f32[1,8]{1,0:T(1,128)S(1)} %copy-done.12, bf16[2,32,128]{2,1,0:T(8,128)(2,1)S(1)} %copy-done.8, ...), custom_call_target="tpu_custom_call" | custom-call | flops 1000000000 | bytes 20000000 | tf_op jit(solution)/shard_map/pallas_call | solution.py:209
  37.4 0.0 copy-start.4
  37.5 30.8 %shard_map.123 = (bf16[8,16,64,128]{3,2,1,0:T(8,128)(2,1)S(1)}, f32[4,16,8,32]{3,2,1,0:T(8,128)S(1)}) custom-call(bf16[8,16,64,128]{3,2,1,0:T(8,128)(2,1)} %refs_0_.1, f32[8,16,64,128]{3,2,1,0:T(8,128)} %get-tuple-element.8.refs_1_, f32[16,4,8,8,32]{4,3,2,1,0:T(8,128)} %bitcast.20, f32[8,8]{1,0:T(8,128)S(1)} %bitcast.17, bf16[2,32,128]{2,1,0:T(8,128)(2,1)S(1)} %copy-done.9, ...), custom_call_target="tpu_custom_call" | custom-call | flops 1000000000 | bytes 20000000 | tf_op jit(solution)/shard_map/pallas_call | solution.py:209
  68.3 0.0 copy-start.5
  68.3 0.7 copy-done.5
  69.0 1.3 collective-permute-start
  70.3 49.0 %collective-permute-done.refs_0_ = bf16[8,16,64,128]{3,2,1,0:T(8,128)(2,1)} collective-permute-done((bf16[8,16,64,128]{3,2,1,0:T(8,128)(2,1)S(1)}, bf16[8,16,64,128]{3,2,1,0:T(8,128)(2,1)}, u32[]{:S(2)}, u32[]{:S(2)}) %collective-permute-start) | collective-permute-done | bytes 2097184 | tf_op jit(solution)/shard_map/ppermute | solution.py:20
  119.3 28.9 %shard_map.124 = (bf16[8,16,64,128]{3,2,1,0:T(8,128)(2,1)S(1)}, f32[4,16,8,32]{3,2,1,0:T(8,128)S(1)}) custom-call(bf16[8,16,64,128]{3,2,1,0:T(8,128)(2,1)} %collective-permute-done.refs_0_, f32[8,16,64,128]{3,2,1,0:T(8,128)} %get-tuple-element.8.refs_1_, f32[16,4,8,8,32]{4,3,2,1,0:T(8,128)} %bitcast.21, f32[8,8]{1,0:T(8,128)S(1)} %bitcast.18, ...), custom_call_target="tpu_custom_call" | custom-call | flops 1000000000 | bytes 20000000 | tf_op jit(solution)/shard_map/pallas_call | solution.py:209
  148.3 0.0 copy-start.6
  148.3 1.5 %select_bitcast_fusion = bf16[1,8,16,64,128]{4,3,2,1,0:T(8,128)(2,1)} fusion(bf16[8,16,64,128]{3,2,1,0:T(8,128)(2,1)S(1)} %get-tuple-element.10, bf16[8,16,64,128]{3,2,1,0:T(8,128)(2,1)S(1)} %get-tuple-element.9, pred[]{:T(512)S(6)} %eq.7, pred[]{:T(512)S(6)} %eq.6), kind=kLoop, calls=%fused_computation | loop fusion | flops 2097152 | bytes 6291458 | tf_op jit(solution)/shard_map/broadcast_in_dim | solution.py:286
  149.9 1.7 %broadcast_multiply_fusion = f32[1,16,4,8,8,32]{5,4,3,2,1,0:T(8,128)} fusion(f32[4,16,8,32]{3,2,1,0:T(8,128)S(1)} %get-tuple-element.11, f32[16,4,8,32]{3,2,0,1:T(8,128)S(1)} %select_bitcast_fusion.1), kind=kLoop, calls=%fused_computation.1 | loop fusion | flops 131072 | bytes 655360 | tf_op jit(solution)/shard_map/mul | solution.py:285
  (12 shorter events, 0.0 us)
Async XLA Ops:
  0.6 2.4 %copy-start.7 = (bf16[96,128]{1,0:T(8,128)(2,1)S(1)}, bf16[96,128]{1,0:T(8,128)(2,1)}, u32[]{:S(2)}) copy-start(bf16[96,128]{1,0:T(8,128)(2,1)} %constant.38.clone.refs_5_) | copy-start | bytes 73732
  0.6 2.4 %copy-start = (bf16[1,8,16,64,128]{4,3,2,1,0:T(8,128)(2,1)S(1)}, bf16[1,8,16,64,128]{4,3,2,1,0:T(8,128)(2,1)}, u32[]{:S(2)}) copy-start(bf16[1,8,16,64,128]{4,3,2,1,0:T(8,128)(2,1)} %param.11) | copy-start | bytes 6291460
  0.7 2.4 %copy-start.12 = (f32[1,8]{1,0:T(1,128)S(1)}, f32[1,8]{1,0:T(1,128)}, u32[]{:S(2)}) copy-start(f32[1,8]{1,0:T(1,128)} %refs_3_.1) | copy-start | bytes 100
  3.0 0.8 copy-start.1
  3.9 0.8 copy-start.3
  4.6 0.7 copy-start.8
  5.3 0.7 copy-start.10
  6.0 31.4 %copy-start.2 = (bf16[2,128,32]{2,1,0:T(8,128)(2,1)S(1)}, bf16[2,128,32]{2,1,0:T(8,128)(2,1)}, u32[]{:S(2)}) copy-start(bf16[2,128,32]{2,1,0:T(8,128)(2,1)} %constant.40.clone.refs_9_) | copy-start | bytes 49156
  6.0 31.4 %copy-start.9 = (bf16[2,32,128]{2,1,0:T(8,128)(2,1)S(1)}, bf16[2,32,128]{2,1,0:T(8,128)(2,1)}, u32[]{:S(2)}) copy-start(bf16[2,32,128]{2,1,0:T(8,128)(2,1)} %constant.37.clone.refs_4_) | copy-start | bytes 49156
  6.0 31.4 %copy-start.11 = (f32[1,8,8]{2,1,0:T(8,128)S(1)}, f32[1,8,8]{2,1,0:T(8,128)}, u32[]{:S(2)}) copy-start(f32[1,8,8]{2,1,0:T(8,128)} %param.14) | copy-start | bytes 772
  37.4 81.9 %copy-start.4 = (bf16[2,32,256]{2,1,0:T(8,128)(2,1)S(1)}, bf16[2,32,256]{2,1,0:T(8,128)(2,1)}, u32[]{:S(2)}) copy-start(bf16[2,32,256]{2,1,0:T(8,128)(2,1)} %constant.39.clone.refs_8_) | copy-start | bytes 98308
  68.3 0.7 copy-start.5
  69.0 50.3 %collective-permute-start = (bf16[8,16,64,128]{3,2,1,0:T(8,128)(2,1)S(1)}, bf16[8,16,64,128]{3,2,1,0:T(8,128)(2,1)}, u32[]{:S(2)}, u32[]{:S(2)}) collective-permute-start(bf16[8,16,64,128]{3,2,1,0:T(8,128)(2,1)S(1)} %get-tuple-element.9), channel_id=1, source_target_pairs={{1,0},{3,2},{5,4},{7,6},{9,8},{11,10},{13,12},{15,14},{17,16},{19,... | collective-permute-start | bytes 6291464 | tf_op jit(solution)/shard_map/ppermute | solution.py:20
  148.3 1.6 %copy-start.6 = (f32[4,16,8,32]{3,2,1,0:T(8,128)S(1)}, f32[4,16,8,32]{3,2,1,0:T(8,128)}, u32[]{:S(2)}) copy-start(f32[4,16,8,32]{3,2,1,0:T(8,128)} %copy-done.5) | copy-start | bytes 196612

commit v2 on v1

--- a/solution.py
+++ b/solution.py
@@ -53,10 +53,10 @@
 ):
     if back:
         (inc_ref, slope_ref, w_hbm, mix_ref, bz_ref, bzs_ref, ky_ref, kyt_ref, bx_ref, bxr_ref,
-         out_ref, modes_ref, *scratch) = refs
+         out_ref, modes_ref, got_ref, *scratch) = refs
     else:
         (inc_ref, w_hbm, mix_ref, bias_ref, bz_ref, bzs_ref, ky_ref, kyt_ref, bx_ref, bxr_ref,
-         out_ref, modes_ref, *scratch) = refs
+         out_ref, modes_ref, got_ref, *scratch) = refs
     (w_ref, sig_ref, ghi_ref, glo_ref, s_ref, r_ref, m_ref, p_ref, q_ref, qs_ref,
      send1, recv1, send2, recv2, wsem) = scratch
     channels, _, yr, zr = inc_ref.shape
@@ -165,6 +165,7 @@
     got = [q_ref[h * nx : (h + 1) * nx].reshape(MODES, xp, lanes) for h in range(ny)]
     got = jnp.concatenate(got, axis=2).astype(f32)
     got = jnp.swapaxes(got, 0, 1)[:xr].reshape(xr * MODES, ny * lanes).astype(bf16)
+    got_ref[...] = got
     qs_ref[...] = dot(got, kyt_ref[0]) + dot(got, kyt_ref[1])
 
     def finish_field(x, carry):
@@ -189,6 +190,58 @@
         return carry
 
     lax.fori_loop(0, xr, finish_field, 0)
+
+
+def ahead_kernel(
+    act_ref, cot_ref, got_ref, got_back_ref, mix_ref, bias_ref, bzs_ref, kyt_ref, out_ref,
+    pre_ref, back_ref,
+):
+    channels, xr, yr, zr = act_ref.shape
+    pre_ref[...] = dot(got_ref[...], kyt_ref[0]) + dot(got_ref[...], kyt_ref[1])
+    back_ref[...] = dot(got_back_ref[...], kyt_ref[0]) + dot(got_back_ref[...], kyt_ref[1])
+
+    def field_of(ref, x):
+        rows = pl.ds(pl.multiple_of(x * MODES, MODES), MODES)
+        top, rest = split(ref[rows, :])
+        stack = jnp.concatenate([top, rest, top], axis=0)
+        return dot(stack, bzs_ref[...], 0, 0).reshape(channels, yr, zr)
+
+    def step(x, carry):
+        field = field_of(pre_ref, x)
+        values = [act_ref[i, x].astype(f32) for i in range(channels)]
+        signals = []
+        for o in range(channels):
+            total = field[o]
+            for i in range(channels):
+                total = total + mix_ref[o, i] * values[i]
+            total = total + bias_ref[0, o]
+            cdf = 0.5 * (1.0 + lax.erf(total * 0.7071067811865476))
+            slope = cdf + total * jnp.exp(-0.5 * total * total) * 0.3989422804014327
+            signals.append(cot_ref[o, x].astype(f32) * slope)
+        field = field_of(back_ref, x)
+        for o in range(channels):
+            total = field[o]
+            for i in range(channels):
+                total = total + mix_ref[i, o] * signals[i]
+            out_ref[o, x] = total.astype(bf16)
+        return carry
+
+    lax.fori_loop(0, xr, step, 0)
+
+
+def ahead(activations, cotangent, got, got_back, mixing, bias, bzs, kyt):
+    channels, xr, yr, zr = activations.shape
+    vmem = pl.BlockSpec(memory_space=pltpu.VMEM)
+    smem = pl.BlockSpec(memory_space=pltpu.SMEM)
+    return pl.pallas_call(
+        ahead_kernel,
+        out_shape=jax.ShapeDtypeStruct(activations.shape, bf16),
+        in_specs=[vmem] * 4 + [smem] * 2 + [vmem] * 2,
+        out_specs=vmem,
+        scratch_shapes=[pltpu.VMEM((xr * MODES, channels * yr), f32)] * 2,
+        compiler_params=pltpu.CompilerParams(vmem_limit_bytes=50 * 2**20),
+        cost_estimate=pl.CostEstimate(flops=10**9, bytes_accessed=10**7, transcendentals=10**6),
+    )(activations, cotangent, got, got_back, mixing, bias, bzs, kyt)
 
 
 def block_turn(back, nx, ny, collective, field, slope, weights, mixing, bias, tables):
@@ -211,9 +264,10 @@
         out_shape=(
             jax.ShapeDtypeStruct(field.shape, bf16 if back else f32),
             jax.ShapeDtypeStruct((cl, jl, channels, MODES), f32),
+            jax.ShapeDtypeStruct((xr * MODES, ny * lanes), bf16),
         ),
         in_specs=specs,
-        out_specs=(vmem, vmem),
+        out_specs=(vmem, vmem, vmem),
         scratch_shapes=[
             pltpu.VMEM(weights.shape, f32),
             pltpu.VMEM(field.shape if back else (8, 128), f32),
@@ -263,9 +317,11 @@
     )
     weights = spectral_weights[0]
     mixing = pointwise[0]
-    slope, input_modes = block_turn(
+    following = [from_behind(v, "segment", -1) for v in (inputs, mixing, channel_bias)]
+    slope, input_modes, got = block_turn(
         False, nx, ny, 0, inputs, None, weights, mixing, channel_bias, tables
     )
+    next_got = from_behind(got, "segment", -1)
     segment_index = lax.axis_index("segment")
     segment_count = lax.axis_size("segment")
     incoming = cotangent
@@ -273,12 +329,18 @@
     kept_modes = jnp.zeros(input_modes.shape, f32)
     for turn_index in range(segment_count):
         active = segment_index == segment_count - 1 - turn_index
-        input_grad, grad_modes = block_turn(
+        input_grad, grad_modes, got_back = block_turn(
             True, nx, ny, 1 + turn_index, incoming, slope, weights, mixing, None, tables
         )
         kept_grad = jnp.where(active, input_grad, kept_grad)
         kept_modes = jnp.where(active, grad_modes, kept_modes)
-        if turn_index + 1 < segment_count:
+        if turn_index == 0 and segment_count > 1:
+            next_back = from_behind(got_back, "segment", -1)
+            incoming = ahead(
+                following[0], cotangent, next_got, next_back, following[1], following[2],
+                tables[1], tables[3],
+            )
+        elif turn_index + 1 < segment_count:
             incoming = from_behind(input_grad, "segment", -1)
     input_modes = jnp.swapaxes(input_modes, 0, 1)
     kept_modes = jnp.swapaxes(kept_modes, 0, 1)

time: 152 us -> 137 us (0.901)
  waiting for transfers between devices: 49 us -> 12.4 us
  Pallas kernels: 91.1 us -> 107 us
  starting transfers between devices: 1.28 us -> 6.58 us
    ppermute x1 -> x5, waiting for transfers between devices: 49 us -> 12.4 us  [from_behind(): return lax.ppermute(block, axis, route)]
    pallas_call x0 -> x1, Pallas kernels: none -> 12.9 us  [ahead(): pl.pallas_call(ahead_kernel, out_shape=jax.ShapeDtypeStruct(activations.s...]
    ppermute x1 -> x5, starting transfers between devices: 1.28 us -> 6.58 us  [from_behind(): return lax.ppermute(block, axis, route)]
    pallas_call x3, Pallas kernels: 91.1 us -> 93.9 us  [block_turn(): pl.pallas_call(functools.partial(kernel, back, nx, ny, xr), out_shape=(ja...]
    unnamed x26 -> x24, local copies, waits for them, and re-layouts: 3.73 us -> 4.36 us
  transfers between devices with their start and end apart: 1 -> 5, of which waited for: 1 -> 1; matrix products, arithmetic and copies ran while one was open for 0% -> 2% of each run, Pallas kernels for 0% -> 46%
where the time goes in v2:
time: 137 us; the launch traced here: 136 us
  Pallas kernels  107 us (78%)
  waiting for transfers between devices  12.4 us (9%)
  starting transfers between devices  6.58 us (5%)
  local copies, waits for them, and re-layouts  6.52 us (5%)
  other arithmetic  3.23 us (2%)
    pallas_call x3, Pallas kernels, block_turn(): pl.pallas_call(functools.partial(kernel, back, nx, ny, xr), out_shape=(ja...  93.9 us
    pallas_call x1, Pallas kernels, ahead(): pl.pallas_call(ahead_kernel, out_shape=jax.ShapeDtypeStruct(activations.s...  12.9 us
    ppermute x5, waiting for transfers between devices, from_behind(): return lax.ppermute(block, axis, route)  12.4 us
    ppermute x5, starting transfers between devices, from_behind(): return lax.ppermute(block, axis, route)  6.58 us
    unnamed x24, local copies, waits for them, and re-layouts  4.36 us
  transfers between devices with their start and end apart: 5, of which 1 were waited for; matrix products, arithmetic and copies ran while one was open for 2% of the time, Pallas kernels for 46%

profile of v2, /device:TPU:0, one launch (start us, length us, event | category | flops | bytes accessed | tf_op | source)
XLA Modules:
  0.0 136.4 jit_solution(1645224405200824689)
XLA Ops:
  0.6 0.0 copy-start.4
  0.7 1.4 %collective-permute-start = (bf16[8,16,64,128]{3,2,1,0:T(8,128)(2,1)}, bf16[8,16,64,128]{3,2,1,0:T(8,128)(2,1)}, u32[]{:S(2)}, u32[]{:S(2)}) collective-permute-start(bf16[8,16,64,128]{3,2,1,0:T(8,128)(2,1)} %bitcast.15), channel_id=1, source_target_pairs={{1,0},{3,2},{5,4},{7,6},{9,8},{11,10},{13,12},{15,14},{17,16},{19,... | collective-permute-start | bytes 6291464 | tf_op jit(solution)/shard_map/ppermute | solution.py:20
  2.1 1.1 dynamic-slice_bitcast_fusion.refs_7_.kyt_ref
  3.2 1.1 dynamic-slice_bitcast_fusion.1.refs_6_
  4.3 0.0 copy-start.2
  4.3 0.8 copy-done.2
  5.1 0.8 copy-done.5
  5.9 0.7 copy-done.9
  6.6 31.8 %shard_map.122 = (f32[8,16,64,128]{3,2,1,0:T(8,128)}, f32[4,16,8,32]{3,2,1,0:T(8,128)S(1)}, bf16[512,256]{1,0:T(8,128)(2,1)}) custom-call(bf16[8,16,64,128]{3,2,1,0:T(8,128)(2,1)S(1)} %bitcast.16, f32[16,4,8,8,32]{4,3,2,1,0:T(8,128)} %bitcast.17, f32[8,8]{1,0:T(8,128)} %bitcast.2.refs_2_.refs_3_, f32[1,8]{1,0:T(1,128)S(1)} %copy-done.11, ...), custom_call_target="tpu_custom_call" | custom-call | flops 1000000000 | bytes 20000000 | tf_op jit(solution)/shard_map/pallas_call | solution.py:262
  38.4 31.6 %shard_map.123 = (bf16[8,16,64,128]{3,2,1,0:T(8,128)(2,1)S(1)}, f32[4,16,8,32]{3,2,1,0:T(8,128)S(1)}, bf16[512,256]{1,0:T(8,128)(2,1)}) custom-call(bf16[8,16,64,128]{3,2,1,0:T(8,128)(2,1)} %cot_ref.1, f32[8,16,64,128]{3,2,1,0:T(8,128)} %get-tuple-element.11.refs_1_, f32[16,4,8,8,32]{4,3,2,1,0:T(8,128)} %bitcast.18, f32[8,8]{1,0:T(8,128)} %bitcast.2.refs_2_.refs_3_, ...), custom_call_target="tpu_custom_call" | custom-call | flops 1000000000 | bytes 20000000 | tf_op jit(solution)/shard_map/pallas_call | solution.py:262
  70.0 0.0 copy-start.7
  70.0 0.7 copy-done.7
  70.7 1.3 collective-permute-start.2
  72.0 1.3 collective-permute-start.1
  73.3 1.3 collective-permute-start.3
  74.6 1.3 collective-permute-start.4
  75.9 0.0 copy-start.6
  75.9 0.0 copy-start.10
  75.9 12.4 %collective-permute-done.4.bias_ref = f32[1,8]{1,0:T(1,128)S(1)} collective-permute-done((f32[1,8]{1,0:T(1,128)S(1)}, f32[1,8]{1,0:T(1,128)S(1)}, u32[]{:S(2)}, u32[]{:S(2)}) %collective-permute-start.4) | collective-permute-done | bytes 64 | tf_op jit(solution)/shard_map/ppermute | solution.py:20
  88.3 12.9 %shard_map.124.refs_0_ = bf16[8,16,64,128]{3,2,1,0:T(8,128)(2,1)S(1)} custom-call(bf16[8,16,64,128]{3,2,1,0:T(8,128)(2,1)} %collective-permute-done.act_ref, bf16[8,16,64,128]{3,2,1,0:T(8,128)(2,1)} %cot_ref.1, bf16[512,256]{1,0:T(8,128)(2,1)} %collective-permute-done.1.got_ref, bf16[512,256]{1,0:T(8,128)(2,1)} %collective-permute-done.2.got_back_ref, ...), custom_call_target="tpu_custom_call" | custom-call | flops 1000000000 | bytes 10000000 | tf_op jit(solution)/shard_map/pallas_call | solution.py:236
  101.3 1.3 copy-done
  102.6 30.5 %shard_map.125 = (bf16[8,16,64,128]{3,2,1,0:T(8,128)(2,1)S(1)}, f32[4,16,8,32]{3,2,1,0:T(8,128)S(1)}, bf16[512,256]{1,0:T(8,128)(2,1)}) custom-call(bf16[8,16,64,128]{3,2,1,0:T(8,128)(2,1)} %copy-done, f32[8,16,64,128]{3,2,1,0:T(8,128)} %get-tuple-element.11.refs_1_, f32[16,4,8,8,32]{4,3,2,1,0:T(8,128)} %bitcast.19, f32[8,8]{1,0:T(8,128)} %bitcast.2.refs_2_.refs_3_, ...), custom_call_target="tpu_custom_call" | custom-call | flops 1000000000 | bytes 20000000 | tf_op jit(solution)/shard_map/pallas_call | solution.py:262
  133.2 1.7 %broadcast_multiply_fusion = f32[1,16,4,8,8,32]{5,4,3,2,1,0:T(8,128)} fusion(f32[4,16,8,32]{3,2,1,0:T(8,128)S(1)} %get-tuple-element.15, f32[16,4,8,32]{3,2,0,1:T(8,128)S(1)} %select_bitcast_fusion.1), kind=kLoop, calls=%fused_computation.1 | loop fusion | flops 131072 | bytes 655360 | tf_op jit(solution)/shard_map/mul | solution.py:347
  134.8 1.5 %select_bitcast_fusion = bf16[1,8,16,64,128]{4,3,2,1,0:T(8,128)(2,1)} fusion(bf16[8,16,64,128]{3,2,1,0:T(8,128)(2,1)S(1)} %get-tuple-element.13, bf16[8,16,64,128]{3,2,1,0:T(8,128)(2,1)S(1)} %get-tuple-element.14, pred[]{:T(512)S(6)} %eq.7, pred[]{:T(512)S(6)} %eq.6), kind=kLoop, calls=%fused_computation | loop fusion | flops 2097152 | bytes 6291458 | tf_op jit(solution)/shard_map/broadcast_in_dim | solution.py:348
  (19 shorter events, 0.1 us)
Async XLA Ops:
  0.6 3.6 %copy-start.4 = (bf16[96,128]{1,0:T(8,128)(2,1)S(1)}, bf16[96,128]{1,0:T(8,128)(2,1)}, u32[]{:S(2)}) copy-start(bf16[96,128]{1,0:T(8,128)(2,1)} %constant.38.clone.refs_5_.bzs_ref) | copy-start | bytes 73732
  0.6 3.6 %copy-start.1 = (bf16[1,8,16,64,128]{4,3,2,1,0:T(8,128)(2,1)S(1)}, bf16[1,8,16,64,128]{4,3,2,1,0:T(8,128)(2,1)}, u32[]{:S(2)}) copy-start(bf16[1,8,16,64,128]{4,3,2,1,0:T(8,128)(2,1)} %param.11) | copy-start | bytes 6291460
  0.7 3.6 %copy-start.11 = (f32[1,8]{1,0:T(1,128)S(1)}, f32[1,8]{1,0:T(1,128)}, u32[]{:S(2)}) copy-start(f32[1,8]{1,0:T(1,128)} %refs_3_.1) | copy-start | bytes 100
  0.7 87.7 %collective-permute-start = (bf16[8,16,64,128]{3,2,1,0:T(8,128)(2,1)}, bf16[8,16,64,128]{3,2,1,0:T(8,128)(2,1)}, u32[]{:S(2)}, u32[]{:S(2)}) collective-permute-start(bf16[8,16,64,128]{3,2,1,0:T(8,128)(2,1)} %bitcast.15), channel_id=1, source_target_pairs={{1,0},{3,2},{5,4},{7,6},{9,8},{11,10},{13,12},{15,14},{17,16},{19,... | collective-permute-start | bytes 6291464 | tf_op jit(solution)/shard_map/ppermute | solution.py:20
  4.3 0.8 copy-start.2
  5.1 0.8 copy-start.5
  5.9 0.7 copy-start.9
  6.6 31.8 %copy-start.3 = (bf16[2,128,32]{2,1,0:T(8,128)(2,1)S(1)}, bf16[2,128,32]{2,1,0:T(8,128)(2,1)}, u32[]{:S(2)}) copy-start(bf16[2,128,32]{2,1,0:T(8,128)(2,1)} %constant.40.clone.refs_9_) | copy-start | bytes 49156
  70.0 0.7 copy-start.7
  70.7 17.6 %collective-permute-start.2 = (bf16[512,256]{1,0:T(8,128)(2,1)}, bf16[512,256]{1,0:T(8,128)(2,1)}, u32[]{:S(2)}, u32[]{:S(2)}) collective-permute-start(bf16[512,256]{1,0:T(8,128)(2,1)} %get-tuple-element.12), channel_id=1, source_target_pairs={{1,0},{3,2},{5,4},{7,6},{9,8},{11,10},{13,12},{15,14},{17,16},{19,... | collective-permute-start | bytes 786440 | tf_op jit(solution)/shard_map/ppermute | solution.py:20
  72.0 16.3 %collective-permute-start.1 = (bf16[512,256]{1,0:T(8,128)(2,1)}, bf16[512,256]{1,0:T(8,128)(2,1)}, u32[]{:S(2)}, u32[]{:S(2)}) collective-permute-start(bf16[512,256]{1,0:T(8,128)(2,1)} %get-tuple-element.10), channel_id=1, source_target_pairs={{1,0},{3,2},{5,4},{7,6},{9,8},{11,10},{13,12},{15,14},{17,16},{19,... | collective-permute-start | bytes 786440 | tf_op jit(solution)/shard_map/ppermute | solution.py:20
  73.3 15.0 %collective-permute-start.3 = (f32[8,8]{1,0:T(8,128)}, f32[8,8]{1,0:T(8,128)S(1)}, u32[]{:S(2)}, u32[]{:S(2)}) collective-permute-start(f32[8,8]{1,0:T(8,128)} %bitcast.2.refs_2_.refs_3_), channel_id=1, source_target_pairs={{1,0},{3,2},{5,4},{7,6},{9,8},{11,10},{13,12},{15,14},{17,16},{19,... | collective-permute-start | bytes 776 | tf_op jit(solution)/shard_map/ppermute | solution.py:20
  74.6 13.7 %collective-permute-start.4 = (f32[1,8]{1,0:T(1,128)S(1)}, f32[1,8]{1,0:T(1,128)S(1)}, u32[]{:S(2)}, u32[]{:S(2)}) collective-permute-start(f32[1,8]{1,0:T(1,128)S(1)} %copy-done.11), channel_id=1, source_target_pairs={{1,0},{3,2},{5,4},{7,6},{9,8},{11,10},{13,12},{15,14},{17,16},{19,... | collective-permute-start | bytes 104 | tf_op jit(solution)/shard_map/ppermute | solution.py:20
  75.9 26.7 %copy-start.6 = (bf16[2,32,256]{2,1,0:T(8,128)(2,1)S(1)}, bf16[2,32,256]{2,1,0:T(8,128)(2,1)}, u32[]{:S(2)}) copy-start(bf16[2,32,256]{2,1,0:T(8,128)(2,1)} %constant.39.clone.refs_8_) | copy-start | bytes 98308
  75.9 26.7 %copy-start.10 = (bf16[2,32,128]{2,1,0:T(8,128)(2,1)S(1)}, bf16[2,32,128]{2,1,0:T(8,128)(2,1)}, u32[]{:S(2)}) copy-start(bf16[2,32,128]{2,1,0:T(8,128)(2,1)} %constant.37.clone.refs_4_) | copy-start | bytes 49156
  101.2 1.3 copy-start
  102.6 30.5 %copy-start.8 = (f32[4,16,8,32]{3,2,1,0:T(8,128)S(1)}, f32[4,16,8,32]{3,2,1,0:T(8,128)}, u32[]{:S(2)}) copy-start(f32[4,16,8,32]{3,2,1,0:T(8,128)} %copy-done.7) | copy-start | bytes 196612

commit v3 on v2

--- a/solution.py
+++ b/solution.py
@@ -324,7 +324,9 @@
     next_got = from_behind(got, "segment", -1)
     segment_index = lax.axis_index("segment")
     segment_count = lax.axis_size("segment")
-    incoming = cotangent
+    incoming, following[1], following[2] = lax.optimization_barrier(
+        (cotangent, following[1], following[2])
+    )
     kept_grad = jnp.zeros(cotangent.shape, bf16)
     kept_modes = jnp.zeros(input_modes.shape, f32)
     for turn_index in range(segment_count):

time: 137 us -> 142 us (1.036)
  waiting for transfers between devices: 12.4 us -> 18.7 us
  Pallas kernels: 107 us -> 104 us
    ppermute x5, waiting for transfers between devices: 12.4 us -> 18.7 us  [from_behind(): return lax.ppermute(block, axis, route)]
    pallas_call x3, Pallas kernels: 93.9 us -> 91.3 us  [block_turn(): pl.pallas_call(functools.partial(kernel, back, nx, ny, xr), out_shape=(ja...]
    unnamed x24 -> x28, local copies, waits for them, and re-layouts: 4.36 us -> 5.05 us
  transfers between devices with their start and end apart: 5 -> 5, of which waited for: 1 -> 2; matrix products, arithmetic and copies ran while one was open for 2% -> 2% of each run, Pallas kernels for 46% -> 44%
where the time goes in v3:
time: 142 us; the launch traced here: 141 us
  Pallas kernels  104 us (73%)
  waiting for transfers between devices  18.7 us (13%)
  local copies, waits for them, and re-layouts  7.22 us (5%)
  starting transfers between devices  6.58 us (5%)
  other arithmetic  3.22 us (2%)
    pallas_call x3, Pallas kernels, block_turn(): pl.pallas_call(functools.partial(kernel, back, nx, ny, xr), out_shape=(ja...  91.3 us
    ppermute x5, waiting for transfers between devices, from_behind(): return lax.ppermute(block, axis, route)  18.7 us
    pallas_call x1, Pallas kernels, ahead(): pl.pallas_call(ahead_kernel, out_shape=jax.ShapeDtypeStruct(activations.s...  12.9 us
    ppermute x5, starting transfers between devices, from_behind(): return lax.ppermute(block, axis, route)  6.58 us
    unnamed x28, local copies, waits for them, and re-layouts  5.05 us
  transfers between devices with their start and end apart: 5, of which 2 were waited for; matrix products, arithmetic and copies ran while one was open for 2% of the time, Pallas kernels for 44%

profile of v3, /device:TPU:0, one launch (start us, length us, event | category | flops | bytes accessed | tf_op | source)
XLA Modules:
  0.0 140.7 jit_solution(5648994992120470910)
XLA Ops:
  0.6 0.0 copy-start.4
  0.7 1.4 %collective-permute-start = (bf16[8,16,64,128]{3,2,1,0:T(8,128)(2,1)}, bf16[8,16,64,128]{3,2,1,0:T(8,128)(2,1)}, u32[]{:S(2)}, u32[]{:S(2)}) collective-permute-start(bf16[8,16,64,128]{3,2,1,0:T(8,128)(2,1)} %bitcast.15), channel_id=1, source_target_pairs={{1,0},{3,2},{5,4},{7,6},{9,8},{11,10},{13,12},{15,14},{17,16},{19,... | collective-permute-start | bytes 6291464 | tf_op jit(solution)/shard_map/ppermute | solution.py:20
  2.1 1.3 collective-permute-start.2
  3.4 1.3 collective-permute-start.3
  4.7 1.1 dynamic-slice_bitcast_fusion.refs_7_.kyt_ref
  5.8 1.1 dynamic-slice_bitcast_fusion.1.refs_6_
  6.9 0.0 copy-start.2
  6.9 0.8 copy-done.2
  7.7 0.8 copy-done.5
  8.5 0.7 copy-done.9
  9.2 0.7 copy-done.11
  9.9 31.5 %shard_map.122 = (f32[8,16,64,128]{3,2,1,0:T(8,128)}, f32[4,16,8,32]{3,2,1,0:T(8,128)S(1)}, bf16[512,256]{1,0:T(8,128)(2,1)}) custom-call(bf16[8,16,64,128]{3,2,1,0:T(8,128)(2,1)S(1)} %bitcast.16, f32[16,4,8,8,32]{4,3,2,1,0:T(8,128)} %bitcast.21, f32[8,8]{1,0:T(8,128)S(1)} %bitcast.18, f32[1,8]{1,0:T(1,128)S(1)} %copy-done.13, ...), custom_call_target="tpu_custom_call" | custom-call | flops 1000000000 | bytes 20000000 | tf_op jit(solution)/shard_map/pallas_call | solution.py:262
  41.4 1.3 collective-permute-start.1
  42.7 9.1 %collective-permute-done.3.bias_ref = f32[1,8]{1,0:T(1,128)S(1)} collective-permute-done((f32[1,8]{1,0:T(1,128)}, f32[1,8]{1,0:T(1,128)S(1)}, u32[]{:S(2)}, u32[]{:S(2)}) %collective-permute-start.3) | collective-permute-done | bytes 64 | tf_op jit(solution)/shard_map/ppermute | solution.py:20
  51.8 30.0 %shard_map.123 = (bf16[8,16,64,128]{3,2,1,0:T(8,128)(2,1)S(1)}, f32[4,16,8,32]{3,2,1,0:T(8,128)S(1)}, bf16[512,256]{1,0:T(8,128)(2,1)}) custom-call(bf16[8,16,64,128]{3,2,1,0:T(8,128)(2,1)} %cot_ref.1, f32[8,16,64,128]{3,2,1,0:T(8,128)} %get-tuple-element.15.refs_1_, f32[16,4,8,8,32]{4,3,2,1,0:T(8,128)} %bitcast.22, f32[8,8]{1,0:T(8,128)S(1)} %bitcast.19, ...), custom_call_target="tpu_custom_call" | custom-call | flops 1000000000 | bytes 20000000 | tf_op jit(solution)/shard_map/pallas_call | solution.py:262
  81.9 0.7 copy-done.7
  82.5 1.3 collective-permute-start.4
  83.8 0.0 copy-start.6
  83.9 9.6 %collective-permute-done.4.got_back_ref = bf16[512,256]{1,0:T(8,128)(2,1)} collective-permute-done((bf16[512,256]{1,0:T(8,128)(2,1)}, bf16[512,256]{1,0:T(8,128)(2,1)}, u32[]{:S(2)}, u32[]{:S(2)}) %collective-permute-start.4) | collective-permute-done | bytes 262176 | tf_op jit(solution)/shard_map/ppermute | solution.py:20
  93.5 12.9 %shard_map.124.refs_0_ = bf16[8,16,64,128]{3,2,1,0:T(8,128)(2,1)S(1)} custom-call(bf16[8,16,64,128]{3,2,1,0:T(8,128)(2,1)} %collective-permute-done.act_ref, bf16[8,16,64,128]{3,2,1,0:T(8,128)(2,1)} %cot_ref.1, bf16[512,256]{1,0:T(8,128)(2,1)} %collective-permute-done.1.got_ref, bf16[512,256]{1,0:T(8,128)(2,1)} %collective-permute-done.4.got_back_ref, ...), custom_call_target="tpu_custom_call" | custom-call | flops 1000000000 | bytes 10000000 | tf_op jit(solution)/shard_map/pallas_call | solution.py:236
  106.3 1.3 copy-done
  107.7 29.8 %shard_map.125 = (bf16[8,16,64,128]{3,2,1,0:T(8,128)(2,1)S(1)}, f32[4,16,8,32]{3,2,1,0:T(8,128)S(1)}, bf16[512,256]{1,0:T(8,128)(2,1)}) custom-call(bf16[8,16,64,128]{3,2,1,0:T(8,128)(2,1)} %copy-done, f32[8,16,64,128]{3,2,1,0:T(8,128)} %get-tuple-element.15.refs_1_, f32[16,4,8,8,32]{4,3,2,1,0:T(8,128)} %bitcast.23, f32[8,8]{1,0:T(8,128)S(1)} %bitcast.20, ...), custom_call_target="tpu_custom_call" | custom-call | flops 1000000000 | bytes 20000000 | tf_op jit(solution)/shard_map/pallas_call | solution.py:262
  137.5 1.7 %broadcast_multiply_fusion = f32[1,16,4,8,8,32]{5,4,3,2,1,0:T(8,128)} fusion(f32[4,16,8,32]{3,2,1,0:T(8,128)S(1)} %get-tuple-element.21, f32[16,4,8,32]{3,2,0,1:T(8,128)S(1)} %select_bitcast_fusion.1), kind=kLoop, calls=%fused_computation.1 | loop fusion | flops 131072 | bytes 655360 | tf_op jit(solution)/shard_map/mul | solution.py:349
  139.2 1.5 %select_bitcast_fusion = bf16[1,8,16,64,128]{4,3,2,1,0:T(8,128)(2,1)} fusion(bf16[8,16,64,128]{3,2,1,0:T(8,128)(2,1)S(1)} %get-tuple-element.19, bf16[8,16,64,128]{3,2,1,0:T(8,128)(2,1)S(1)} %get-tuple-element.20, pred[]{:T(512)S(6)} %eq.7, pred[]{:T(512)S(6)} %eq.6), kind=kLoop, calls=%fused_computation | loop fusion | flops 2097152 | bytes 6291458 | tf_op jit(solution)/shard_map/broadcast_in_dim | solution.py:350
  (23 shorter events, 0.1 us)
Async XLA Ops:
  0.6 6.2 %copy-start.4 = (bf16[96,128]{1,0:T(8,128)(2,1)S(1)}, bf16[96,128]{1,0:T(8,128)(2,1)}, u32[]{:S(2)}) copy-start(bf16[96,128]{1,0:T(8,128)(2,1)} %constant.38.clone.refs_5_.bzs_ref) | copy-start | bytes 73732
  0.6 6.2 %copy-start.1 = (bf16[1,8,16,64,128]{4,3,2,1,0:T(8,128)(2,1)S(1)}, bf16[1,8,16,64,128]{4,3,2,1,0:T(8,128)(2,1)}, u32[]{:S(2)}) copy-start(bf16[1,8,16,64,128]{4,3,2,1,0:T(8,128)(2,1)} %param.11) | copy-start | bytes 6291460
  0.7 6.2 %copy-start.13 = (f32[1,8]{1,0:T(1,128)S(1)}, f32[1,8]{1,0:T(1,128)}, u32[]{:S(2)}) copy-start(f32[1,8]{1,0:T(1,128)} %refs_3_.1) | copy-start | bytes 100
  0.7 92.8 %collective-permute-start = (bf16[8,16,64,128]{3,2,1,0:T(8,128)(2,1)}, bf16[8,16,64,128]{3,2,1,0:T(8,128)(2,1)}, u32[]{:S(2)}, u32[]{:S(2)}) collective-permute-start(bf16[8,16,64,128]{3,2,1,0:T(8,128)(2,1)} %bitcast.15), channel_id=1, source_target_pairs={{1,0},{3,2},{5,4},{7,6},{9,8},{11,10},{13,12},{15,14},{17,16},{19,... | collective-permute-start | bytes 6291464 | tf_op jit(solution)/shard_map/ppermute | solution.py:20
  2.1 49.7 %collective-permute-start.2 = (f32[8,8]{1,0:T(8,128)}, f32[8,8]{1,0:T(8,128)S(1)}, u32[]{:S(2)}, u32[]{:S(2)}) collective-permute-start(f32[8,8]{1,0:T(8,128)} %bitcast.17), channel_id=1, source_target_pairs={{1,0},{3,2},{5,4},{7,6},{9,8},{11,10},{13,12},{15,14},{17,16},{19,... | collective-permute-start | bytes 776 | tf_op jit(solution)/shard_map/ppermute | solution.py:20
  3.4 48.4 %collective-permute-start.3 = (f32[1,8]{1,0:T(1,128)}, f32[1,8]{1,0:T(1,128)S(1)}, u32[]{:S(2)}, u32[]{:S(2)}) collective-permute-start(f32[1,8]{1,0:T(1,128)} %refs_3_.1), channel_id=1, source_target_pairs={{1,0},{3,2},{5,4},{7,6},{9,8},{11,10},{13,12},{15,14},{17,16},{19,... | collective-permute-start | bytes 104 | tf_op jit(solution)/shard_map/ppermute | solution.py:20
  6.9 0.8 copy-start.2
  7.7 0.8 copy-start.5
  8.5 0.7 copy-start.9
  9.2 0.7 copy-start.11
  9.9 41.9 %copy-start.3 = (bf16[2,128,32]{2,1,0:T(8,128)(2,1)S(1)}, bf16[2,128,32]{2,1,0:T(8,128)(2,1)}, u32[]{:S(2)}) copy-start(bf16[2,128,32]{2,1,0:T(8,128)(2,1)} %constant.40.clone.refs_9_) | copy-start | bytes 49156
  41.4 42.5 %collective-permute-start.1 = (bf16[512,256]{1,0:T(8,128)(2,1)}, bf16[512,256]{1,0:T(8,128)(2,1)}, u32[]{:S(2)}, u32[]{:S(2)}) collective-permute-start(bf16[512,256]{1,0:T(8,128)(2,1)} %get-tuple-element.13), channel_id=1, source_target_pairs={{1,0},{3,2},{5,4},{7,6},{9,8},{11,10},{13,12},{15,14},{17,16},{19,... | collective-permute-start | bytes 786440 | tf_op jit(solution)/shard_map/ppermute | solution.py:20
  81.8 0.7 copy-start.7
  82.5 10.9 %collective-permute-start.4 = (bf16[512,256]{1,0:T(8,128)(2,1)}, bf16[512,256]{1,0:T(8,128)(2,1)}, u32[]{:S(2)}, u32[]{:S(2)}) collective-permute-start(bf16[512,256]{1,0:T(8,128)(2,1)} %get-tuple-element.16), channel_id=1, source_target_pairs={{1,0},{3,2},{5,4},{7,6},{9,8},{11,10},{13,12},{15,14},{17,16},{19,... | collective-permute-start | bytes 786440 | tf_op jit(solution)/shard_map/ppermute | solution.py:20
  83.8 23.8 %copy-start.6 = (bf16[2,32,256]{2,1,0:T(8,128)(2,1)S(1)}, bf16[2,32,256]{2,1,0:T(8,128)(2,1)}, u32[]{:S(2)}) copy-start(bf16[2,32,256]{2,1,0:T(8,128)(2,1)} %constant.39.clone.refs_8_) | copy-start | bytes 98308
  83.9 23.8 %copy-start.10 = (bf16[2,32,128]{2,1,0:T(8,128)(2,1)S(1)}, bf16[2,32,128]{2,1,0:T(8,128)(2,1)}, u32[]{:S(2)}) copy-start(bf16[2,32,128]{2,1,0:T(8,128)(2,1)} %constant.37.clone.refs_4_) | copy-start | bytes 49156
  83.9 23.8 %copy-start.12 = (f32[1,8,8]{2,1,0:T(8,128)S(1)}, f32[1,8,8]{2,1,0:T(8,128)}, u32[]{:S(2)}) copy-start(f32[1,8,8]{2,1,0:T(8,128)} %param.14) | copy-start | bytes 772
  106.3 1.3 copy-start
  107.7 29.8 %copy-start.8 = (f32[4,16,8,32]{3,2,1,0:T(8,128)S(1)}, f32[4,16,8,32]{3,2,1,0:T(8,128)}, u32[]{:S(2)}) copy-start(f32[4,16,8,32]{3,2,1,0:T(8,128)} %copy-done.7) | copy-start | bytes 196612
